TPU v7x, 128 devices: a whole 4x4x4 slice. The times are simulated.
128 devices in a mesh: segment: 4 (over y_hi, core), seq: 16 (over z, x), tp: 2 (over y_lo).
Axes of the slice: x: 4, y: 4 (y_hi: 2, y_lo: 2; y = y_hi * 2 + y_lo), z: 4, core: 2. Of those that a mesh axis runs over, the one named last changes fastest.
Arguments:
- pairs: bfloat16 [4, 4096, 2, 8192], P('segment', ('seq', 'tp')), may hold values from -4 to 4
- queries: bfloat16 [4, 1536, 8192], P('segment', None, ('seq', 'tp')), may hold values from -24 to 24
- upstream: bfloat16 [4, 1536, 8192], P('segment', None, ('seq', 'tp')), may hold values from -6 to 6
Outputs:
- context: bfloat16 [4, 1536, 8192], P('segment', None, ('seq', 'tp'))
- grad_query: bfloat16 [4, 1536, 8192], P('segment', None, ('seq', 'tp'))
- grad_pairs: bfloat16 [4, 4096, 2, 8192], P('segment', ('seq', 'tp'))
All inputs are finite; a program needn't handle non-finite values.
Results may differ from a plain program's by a relative error of at most 0.011.
Values may be sent and summed in bfloat16 or wider, within the bound.
A program may use at most 128 MiB of HBM per device.

v0:
```python
import jax
import jax.numpy as jnp
from jax import lax
from jax.sharding import PartitionSpec as P

HEAD = 128


def passed_along(block, axis, distance):
    devices = range(lax.axis_size(axis))
    route = [((i - distance) % len(devices), i) for i in devices]
    return lax.ppermute(block, axis, route)


def spread_heads(pairs):
    rows = pairs.shape[1]
    width = pairs.shape[3]
    seq_count = lax.axis_size("seq")
    tp_count = lax.axis_size("tp")
    local = width // (seq_count * tp_count)
    shaped = pairs.reshape(1, rows, 2, seq_count * tp_count, local)
    moved = lax.all_to_all(shaped, ("seq", "tp"), split_axis=3, concat_axis=0, tiled=True)
    return moved.reshape(seq_count * tp_count * rows, 2, local)


def collect_rows(grads):
    seq_count = lax.axis_size("seq")
    tp_count = lax.axis_size("tp")
    groups = seq_count * tp_count
    rows = grads.shape[0] // groups
    local = grads.shape[2]
    shaped = grads.reshape(groups, rows, 2, 1, local)
    moved = lax.all_to_all(shaped, ("seq", "tp"), split_axis=0, concat_axis=3, tiled=True)
    return moved.reshape(1, rows, 2, groups * local)


def attend(head_pairs, query_rows, grad_rows):
    enc_len = head_pairs.shape[0]
    local = head_pairs.shape[2]
    num_heads = local // HEAD
    dec_len = query_rows.shape[0]
    block = min(512, dec_len)
    count = dec_len // block
    factor = HEAD ** (-0.5)
    keys_all = head_pairs[:, 0, :].reshape(enc_len, num_heads, HEAD)
    values_all = head_pairs[:, 1, :].reshape(enc_len, num_heads, HEAD)
    query_blocks = query_rows.reshape(count, block, num_heads, HEAD)
    grad_blocks = grad_rows.reshape(count, block, num_heads, HEAD)

    def step(carry, inputs):
        grad_keys, grad_values = carry
        query_block, grad_block = inputs
        scores = (
            jnp.einsum("bhd,shd->hbs", query_block, keys_all, preferred_element_type=jnp.float32)
            * factor
        )
        row_max = jnp.max(scores, axis=2, keepdims=True)
        raised = jnp.exp(scores - row_max)
        weights = raised / jnp.sum(raised, axis=2, keepdims=True)
        weights_low = weights.astype(jnp.bfloat16)
        full_context = jnp.einsum(
            "hbs,shd->bhd", weights_low, values_all, preferred_element_type=jnp.float32
        )
        row_dot = jnp.sum(grad_block.astype(jnp.float32) * full_context, axis=2)
        grad_weights = jnp.einsum(
            "bhd,shd->hbs", grad_block, values_all, preferred_element_type=jnp.float32
        )
        grad_scores = (weights * (grad_weights - row_dot.T[:, :, None]) * factor).astype(
            jnp.bfloat16
        )
        grad_q = jnp.einsum(
            "hbs,shd->bhd", grad_scores, keys_all, preferred_element_type=jnp.float32
        )
        grad_keys = grad_keys + jnp.einsum(
            "hbs,bhd->shd", grad_scores, query_block, preferred_element_type=jnp.float32
        )
        grad_values = grad_values + jnp.einsum(
            "hbs,bhd->shd", weights_low, grad_block, preferred_element_type=jnp.float32
        )
        return (
            (grad_keys, grad_values),
            (full_context.astype(jnp.bfloat16), grad_q.astype(jnp.bfloat16)),
        )

    zeros_start = jnp.zeros((enc_len, num_heads, HEAD), jnp.float32)
    (grad_keys, grad_values), (context, grad_query) = lax.scan(
        step, (zeros_start, zeros_start), (query_blocks, grad_blocks)
    )
    grad_pairs = (
        jnp.stack([grad_keys, grad_values], axis=1).astype(jnp.bfloat16).reshape(enc_len, 2, local)
    )
    return (context.reshape(dec_len, local), grad_query.reshape(dec_len, local), grad_pairs)


def shards(pairs, queries, upstream):
    arrived = passed_along(pairs, "segment", 1)
    head_pairs = spread_heads(arrived)
    context, grad_query, head_grads = attend(head_pairs, queries[0], upstream[0])
    grad_pairs = passed_along(collect_rows(head_grads), "segment", -1)
    return (context[None], grad_query[None], grad_pairs)


def solution(mesh):
    return jax.shard_map(
        shards,
        mesh=mesh,
        in_specs=(
            P("segment", ("seq", "tp"), None, None),
            P("segment", None, ("seq", "tp")),
            P("segment", None, ("seq", "tp")),
        ),
        out_specs=(
            P("segment", None, ("seq", "tp")),
            P("segment", None, ("seq", "tp")),
            P("segment", ("seq", "tp"), None, None),
        ),
        check_vma=False,
    )
```

profile of v0, /device:TPU:1, one launch (start us, length us, event | category | flops | bytes accessed | tf_op | source)
XLA Modules:
  0.0 413.3 jit_solution(4122751582175901293)
XLA Ops:
  0.6 11.2 %copy.43 = bf16[1,128,2,8192]{1,3,2,0:T(8,128)(2,1)} copy(bf16[1,128,2,8192]{3,2,1,0:T(2,128)(2,1)} %param.5) | data formatting | bytes 8388608 | tf_op args[0]
  11.8 4.3 %collective-permute-start = (bf16[1,128,2,8192]{1,3,2,0:T(8,128)(2,1)}, bf16[1,128,2,8192]{1,3,2,0:T(8,128)(2,1)S(1)}, u32[]{:S(2)}, u32[]{:S(2)}) collective-permute-start(bf16[1,128,2,8192]{1,3,2,0:T(8,128)(2,1)} %copy.43), channel_id=1, source_target_pairs={{96,0},{0,32},{32,64},{64,96},{97,1},{1,33},{33,65},{65,97},{98,2}... | collective-permute-start | bytes 12582920 | tf_op jit(solution)/shard_map/ppermute | solution.py:12
  16.1 45.8 %collective-permute-done = bf16[1,128,2,8192]{1,3,2,0:T(8,128)(2,1)S(1)} collective-permute-done((bf16[1,128,2,8192]{1,3,2,0:T(8,128)(2,1)}, bf16[1,128,2,8192]{1,3,2,0:T(8,128)(2,1)S(1)}, u32[]{:S(2)}, u32[]{:S(2)}) %collective-permute-start) | collective-permute-done | bytes 4194336 | tf_op jit(solution)/shard_map/ppermute | solution.py:12
  61.9 2.2 copy.44
  64.1 8.3 %all-to-all-start = ((bf16[1,128,2,32,256]{1,4,2,0,3:T(8,128)(2,1)}), bf16[1,128,2,32,256]{1,4,2,0,3:T(8,128)(2,1)}, u32[]{:S(2)}, u32[]{:S(2)}) async-start(bf16[1,128,2,32,256]{1,4,2,0,3:T(8,128)(2,1)} %copy.44), calls=%async_computation | async-start | bytes 8388608 | tf_op jit(solution)/shard_map/all_to_all | solution.py:22
  72.6 1.1 reshape_squeeze.14
  73.8 52.5 %all-to-all-done = bf16[1,128,2,32,256]{1,4,2,0,3:T(8,128)(2,1)} async-done(((bf16[1,128,2,32,256]{1,4,2,0,3:T(8,128)(2,1)}), bf16[1,128,2,32,256]{1,4,2,0,3:T(8,128)(2,1)}, u32[]{:S(2)}, u32[]{:S(2)}) %all-to-all-start) | async-done | bytes 4194336 | tf_op jit(solution)/shard_map/all_to_all | solution.py:22
  126.3 6.9 %copy.45 = bf16[32,1,128,2,1,256]{2,0,5,3,4,1:T(8,128)(2,1)} copy(bf16[32,1,128,2,1,256]{2,5,3,0,4,1:T(8,128)(2,1)} %bitcast.2) | data formatting | bytes 8388608 | tf_op jit(solution)/shard_map/all_to_all | solution.py:22
  133.2 7.3 %reshape.54 = bf16[4096,2,256]{0,2,1:T(8,128)(2,1)} reshape(bf16[32,1,128,2,1,256]{2,0,5,3,4,1:T(8,128)(2,1)} %copy.45) | data formatting | bytes 8388608 | tf_op jit(solution)/shard_map/reshape | solution.py:23
  140.5 3.9 fusion.14
  144.4 2.5 copy.47
  146.9 120.2 %while.17 = (s32[]{:T(128)}, f32[4096,2,128]{0,2,1:T(8,128)}, f32[4096,2,128]{0,2,1:T(8,128)}, bf16[3,512,2,128]{3,2,1,0:T(2,128)(2,1)}, bf16[3,512,2,128]{3,2,1...) while((s32[]{:T(128)}, f32[4096,2,128]{0,2,1:T(8,128)}, ...), condition=%wide.region_4.5_spmd.clone, body=%wide.region_0.4_spmd.clone.sunk | while | flops 6489246720 | bytes 213668176 | solution.py:86
  146.9 1.1 constant_dynamic-slice_fusion.4
  148.2 10.3 %fusion.45 = (f32[2,512]{1,0:T(2,128)S(1)}, f32[2,512,4096]{2,1,0:T(8,128)}) fusion(bf16[4096,2,128]{2,0,1:T(8,128)(2,1)} %get-tuple-element.238, bf16[1,512,2,128]{3,2,1,0:T(2,128)(2,1)S(1)} %constant_dynamic-slice_fusion.5), kind=kOutput, calls=%fused_computation.27.clone.1 | convolution fusion | flops 1086328832 | bytes 19140608 | tf_op jit(solution)/shard_map/while/body/eval_jaxpr/sub | solution.py:58
  158.5 7.0 %fusion.46 = bf16[2,512,4096]{2,1,0:T(8,128)(2,1)S(1)} fusion(f32[2,512,4096]{2,1,0:T(8,128)} %get-tuple-element.204, f32[2,512]{1,0:T(2,128)S(1)} %get-tuple-element.205), kind=kLoop, calls=%fused_computation.7.clone.1 | loop fusion | flops 8388608 | bytes 25169920 | tf_op jit(solution)/shard_map/while/body/eval_jaxpr/convert_element_type | solution.py:60
  165.5 2.5 convert_bitcast_fusion.2
  168.0 2.4 fusion.48
  170.4 9.6 %multiply_convert_fusion.2 = bf16[2,512,4096]{2,1,0:T(8,128)(2,1)S(1)} fusion(bf16[4096,2,128]{0,2,1:T(8,128)(2,1)} %get-tuple-element.240, f32[2,512]{1,0:T(2,128)S(1)} %bitcast.118, f32[2,512,4096]{2,1,0:T(8,128)} %get-tuple-element.204, f32[2,512]{1,0:T(2,128)S(1)} %get-tuple-element.205, bf16[1,512,2,128]{3,2,1,0:T(2,128)(2,1)S(1)} %constant_dynamic-slice_fusion.4), kind=kOutput, calls=%fused_computation.1.clone.1 | convolution fusion | flops 1094713344 | bytes 27533312 | tf_op jit(solution)/shard_map/while/body/eval_jaxpr/bhd,shd->hbs/dot_general | solution.py:65
  180.1 2.3 fusion.49
  182.4 2.4 fusion.47
  184.8 1.8 copy_dynamic-update-slice_fusion.3
  188.3 10.3 %fusion.45 = (f32[2,512]{1,0:T(2,128)S(1)}, f32[2,512,4096]{2,1,0:T(8,128)}) fusion(bf16[4096,2,128]{2,0,1:T(8,128)(2,1)} %get-tuple-element.238, bf16[1,512,2,128]{3,2,1,0:T(2,128)(2,1)S(1)} %constant_dynamic-slice_fusion.5), kind=kOutput, calls=%fused_computation.27.clone.1 | convolution fusion | flops 1086328832 | bytes 19140608 | tf_op jit(solution)/shard_map/while/body/eval_jaxpr/sub | solution.py:58
  198.6 7.0 %fusion.46 = bf16[2,512,4096]{2,1,0:T(8,128)(2,1)S(1)} fusion(f32[2,512,4096]{2,1,0:T(8,128)} %get-tuple-element.204, f32[2,512]{1,0:T(2,128)S(1)} %get-tuple-element.205), kind=kLoop, calls=%fused_computation.7.clone.1 | loop fusion | flops 8388608 | bytes 25169920 | tf_op jit(solution)/shard_map/while/body/eval_jaxpr/convert_element_type | solution.py:60
  205.6 2.5 convert_bitcast_fusion.2
  208.1 2.4 fusion.48
  210.5 9.6 %multiply_convert_fusion.2 = bf16[2,512,4096]{2,1,0:T(8,128)(2,1)S(1)} fusion(bf16[4096,2,128]{0,2,1:T(8,128)(2,1)} %get-tuple-element.240, f32[2,512]{1,0:T(2,128)S(1)} %bitcast.118, f32[2,512,4096]{2,1,0:T(8,128)} %get-tuple-element.204, f32[2,512]{1,0:T(2,128)S(1)} %get-tuple-element.205, bf16[1,512,2,128]{3,2,1,0:T(2,128)(2,1)S(1)} %constant_dynamic-slice_fusion.4), kind=kOutput, calls=%fused_computation.1.clone.1 | convolution fusion | flops 1094713344 | bytes 27533312 | tf_op jit(solution)/shard_map/while/body/eval_jaxpr/bhd,shd->hbs/dot_general | solution.py:65
  220.1 2.3 fusion.49
  222.5 2.4 fusion.47
  224.9 1.8 copy_dynamic-update-slice_fusion.3
  227.0 1.1 constant_dynamic-slice_fusion.4
  228.4 10.3 %fusion.45 = (f32[2,512]{1,0:T(2,128)S(1)}, f32[2,512,4096]{2,1,0:T(8,128)}) fusion(bf16[4096,2,128]{2,0,1:T(8,128)(2,1)} %get-tuple-element.238, bf16[1,512,2,128]{3,2,1,0:T(2,128)(2,1)S(1)} %constant_dynamic-slice_fusion.5), kind=kOutput, calls=%fused_computation.27.clone.1 | convolution fusion | flops 1086328832 | bytes 19140608 | tf_op jit(solution)/shard_map/while/body/eval_jaxpr/sub | solution.py:58
  238.7 7.0 %fusion.46 = bf16[2,512,4096]{2,1,0:T(8,128)(2,1)S(1)} fusion(f32[2,512,4096]{2,1,0:T(8,128)} %get-tuple-element.204, f32[2,512]{1,0:T(2,128)S(1)} %get-tuple-element.205), kind=kLoop, calls=%fused_computation.7.clone.1 | loop fusion | flops 8388608 | bytes 25169920 | tf_op jit(solution)/shard_map/while/body/eval_jaxpr/convert_element_type | solution.py:60
  245.7 2.5 convert_bitcast_fusion.2
  248.1 2.4 fusion.48
  250.5 9.6 %multiply_convert_fusion.2 = bf16[2,512,4096]{2,1,0:T(8,128)(2,1)S(1)} fusion(bf16[4096,2,128]{0,2,1:T(8,128)(2,1)} %get-tuple-element.240, f32[2,512]{1,0:T(2,128)S(1)} %bitcast.118, f32[2,512,4096]{2,1,0:T(8,128)} %get-tuple-element.204, f32[2,512]{1,0:T(2,128)S(1)} %get-tuple-element.205, bf16[1,512,2,128]{3,2,1,0:T(2,128)(2,1)S(1)} %constant_dynamic-slice_fusion.4), kind=kOutput, calls=%fused_computation.1.clone.1 | convolution fusion | flops 1094713344 | bytes 27533312 | tf_op jit(solution)/shard_map/while/body/eval_jaxpr/bhd,shd->hbs/dot_general | solution.py:65
  260.2 2.3 fusion.49
  262.6 2.4 fusion.47
  264.9 1.7 copy_dynamic-update-slice_fusion.3
  267.1 2.6 convert.8
  271.3 2.4 pad_maximum_fusion
  273.7 8.4 %copy.51 = bf16[32,128,2,1,256]{4,2,1,3,0:T(2,128)(2,1)} copy(bf16[32,128,2,1,256]{1,0,4,3,2:T(8,128)(2,1)} %pad_maximum_fusion) | data formatting | bytes 8388608 | tf_op jit(solution)/shard_map/stack | solution.py:90
  282.1 52.8 %all_to_all.30 = bf16[32,128,2,1,256]{4,2,1,3,0:T(2,128)(2,1)} all-to-all(bf16[32,128,2,1,256]{4,2,1,3,0:T(2,128)(2,1)} %copy.51), channel_id=1, replica_groups=mesh['segment'=4,'seq'=16,'tp'=2] {'seq','tp'}, dimensions={0} | all-to-all | bytes 8388608 | tf_op jit(solution)/shard_map/all_to_all | solution.py:33
  334.9 11.2 %copy.52 = bf16[32,128,2,1,256]{1,4,0,2,3:T(8,128)(2,1)} copy(bf16[32,128,2,1,256]{4,2,1,3,0:T(2,128)(2,1)} %all_to_all.30) | data formatting | bytes 8388608 | tf_op jit(solution)/shard_map/all_to_all | solution.py:33
  346.1 4.5 %collective-permute-start.1 = (bf16[1,128,2,8192]{1,3,2,0:T(8,128)(2,1)}, bf16[1,128,2,8192]{1,3,2,0:T(8,128)(2,1)}, u32[]{:S(2)}, u32[]{:S(2)}) collective-permute-start(bf16[1,128,2,8192]{1,3,2,0:T(8,128)(2,1)} %bitcast.115), channel_id=1, source_target_pairs={{32,0},{64,32},{96,64},{0,96},{33,1},{65,33},{97,65},{1,97},{34,2}... | collective-permute-start | bytes 12582920 | tf_op jit(solution)/shard_map/ppermute | solution.py:12
  350.6 1.4 broadcast_in_dim_reshape.7
  352.0 1.4 broadcast_in_dim_reshape.6
  353.4 48.8 %collective-permute-done.1 = bf16[1,128,2,8192]{1,3,2,0:T(8,128)(2,1)} collective-permute-done((bf16[1,128,2,8192]{1,3,2,0:T(8,128)(2,1)}, bf16[1,128,2,8192]{1,3,2,0:T(8,128)(2,1)}, u32[]{:S(2)}, u32[]{:S(2)}) %collective-permute-start.1) | collective-permute-done | bytes 4194336 | tf_op jit(solution)/shard_map/ppermute | solution.py:12
  402.2 11.1 %copy.53 = bf16[1,128,2,8192]{3,2,1,0:T(2,128)(2,1)} copy(bf16[1,128,2,8192]{1,3,2,0:T(8,128)(2,1)} %collective-permute-done.1) | data formatting | bytes 8388608
  (58 shorter events, 4.7 us)
Async XLA Ops:
  11.8 50.1 %collective-permute-start = (bf16[1,128,2,8192]{1,3,2,0:T(8,128)(2,1)}, bf16[1,128,2,8192]{1,3,2,0:T(8,128)(2,1)S(1)}, u32[]{:S(2)}, u32[]{:S(2)}) collective-permute-start(bf16[1,128,2,8192]{1,3,2,0:T(8,128)(2,1)} %copy.43), channel_id=1, source_target_pairs={{96,0},{0,32},{32,64},{64,96},{97,1},{1,33},{33,65},{65,97},{98,2}... | collective-permute-start | bytes 12582920 | tf_op jit(solution)/shard_map/ppermute | solution.py:12
  64.1 8.3 %copy-start.7 = (bf16[1,1536,256]{2,1,0:T(8,128)(2,1)S(1)}, bf16[1,1536,256]{2,1,0:T(8,128)(2,1)}, u32[]{:S(2)}) copy-start(bf16[1,1536,256]{2,1,0:T(8,128)(2,1)} %param.6) | copy-start | bytes 2359300
  64.1 8.5 %copy-start.8 = (bf16[1,1536,256]{2,1,0:T(8,128)(2,1)S(1)}, bf16[1,1536,256]{2,1,0:T(8,128)(2,1)}, u32[]{:S(2)}) copy-start(bf16[1,1536,256]{2,1,0:T(8,128)(2,1)} %param.7) | copy-start | bytes 2359300
  64.1 62.2 %all-to-all-start = ((bf16[1,128,2,32,256]{1,4,2,0,3:T(8,128)(2,1)}), bf16[1,128,2,32,256]{1,4,2,0,3:T(8,128)(2,1)}, u32[]{:S(2)}, u32[]{:S(2)}) async-start(bf16[1,128,2,32,256]{1,4,2,0,3:T(8,128)(2,1)} %copy.44), calls=%async_computation | async-start | bytes 8388608 | tf_op jit(solution)/shard_map/all_to_all | solution.py:22
  158.5 7.0 %copy-start.6 = (bf16[4096,2,128]{0,2,1:T(8,128)(2,1)S(1)}, bf16[4096,2,128]{0,2,1:T(8,128)(2,1)}, u32[]{:S(2)}) copy-start(bf16[4096,2,128]{0,2,1:T(8,128)(2,1)} %get-tuple-element.240) | copy-start | bytes 6291460 | tf_op jit(solution)/shard_map/while
  165.5 2.5 copy-start
  170.4 9.7 %copy-start.1 = (f32[4096,2,128]{0,2,1:T(8,128)}, f32[4096,2,128]{0,2,1:T(8,128)S(1)}, u32[]{:S(2)}) copy-start(f32[4096,2,128]{0,2,1:T(8,128)S(1)} %fusion.48) | copy-start | bytes 12582916 | tf_op jit(solution)/shard_map/while
  170.4 9.7 %copy-start.5 = (bf16[4096,2,128]{2,0,1:T(8,128)(2,1)S(1)}, bf16[4096,2,128]{2,0,1:T(8,128)(2,1)}, u32[]{:S(2)}) copy-start(bf16[4096,2,128]{2,0,1:T(8,128)(2,1)} %get-tuple-element.238) | copy-start | bytes 6291460 | tf_op jit(solution)/shard_map/while
  180.1 2.3 copy-start.3
  184.8 2.2 copy-start.4
  198.6 7.0 %copy-start.6 = (bf16[4096,2,128]{0,2,1:T(8,128)(2,1)S(1)}, bf16[4096,2,128]{0,2,1:T(8,128)(2,1)}, u32[]{:S(2)}) copy-start(bf16[4096,2,128]{0,2,1:T(8,128)(2,1)} %get-tuple-element.240) | copy-start | bytes 6291460 | tf_op jit(solution)/shard_map/while
  205.6 2.5 copy-start
  210.5 9.7 %copy-start.1 = (f32[4096,2,128]{0,2,1:T(8,128)}, f32[4096,2,128]{0,2,1:T(8,128)S(1)}, u32[]{:S(2)}) copy-start(f32[4096,2,128]{0,2,1:T(8,128)S(1)} %fusion.48) | copy-start | bytes 12582916 | tf_op jit(solution)/shard_map/while
  210.5 9.7 %copy-start.5 = (bf16[4096,2,128]{2,0,1:T(8,128)(2,1)S(1)}, bf16[4096,2,128]{2,0,1:T(8,128)(2,1)}, u32[]{:S(2)}) copy-start(bf16[4096,2,128]{2,0,1:T(8,128)(2,1)} %get-tuple-element.238) | copy-start | bytes 6291460 | tf_op jit(solution)/shard_map/while
  220.1 2.3 copy-start.3
  224.9 2.2 copy-start.4
  238.7 7.0 %copy-start.6 = (bf16[4096,2,128]{0,2,1:T(8,128)(2,1)S(1)}, bf16[4096,2,128]{0,2,1:T(8,128)(2,1)}, u32[]{:S(2)}) copy-start(bf16[4096,2,128]{0,2,1:T(8,128)(2,1)} %get-tuple-element.240) | copy-start | bytes 6291460 | tf_op jit(solution)/shard_map/while
  245.7 2.5 copy-start
  250.5 9.7 %copy-start.1 = (f32[4096,2,128]{0,2,1:T(8,128)}, f32[4096,2,128]{0,2,1:T(8,128)S(1)}, u32[]{:S(2)}) copy-start(f32[4096,2,128]{0,2,1:T(8,128)S(1)} %fusion.48) | copy-start | bytes 12582916 | tf_op jit(solution)/shard_map/while
  250.5 9.7 %copy-start.5 = (bf16[4096,2,128]{2,0,1:T(8,128)(2,1)S(1)}, bf16[4096,2,128]{2,0,1:T(8,128)(2,1)}, u32[]{:S(2)}) copy-start(bf16[4096,2,128]{2,0,1:T(8,128)(2,1)} %get-tuple-element.238) | copy-start | bytes 6291460 | tf_op jit(solution)/shard_map/while
  260.2 2.3 copy-start.3
  264.9 2.2 copy-start.4
  267.1 3.4 copy-start.2
  334.9 15.7 %copy-start.9 = (bf16[3,512,2,128]{3,2,1,0:T(2,128)(2,1)S(1)}, bf16[3,512,2,128]{3,2,1,0:T(2,128)(2,1)}, u32[]{:S(2)}) copy-start(bf16[3,512,2,128]{3,2,1,0:T(2,128)(2,1)} %get-tuple-element.54) | copy-start | bytes 2359300
  334.9 17.1 %copy-start.10 = (bf16[3,512,2,128]{3,2,1,0:T(2,128)(2,1)S(1)}, bf16[3,512,2,128]{3,2,1,0:T(2,128)(2,1)}, u32[]{:S(2)}) copy-start(bf16[3,512,2,128]{3,2,1,0:T(2,128)(2,1)} %get-tuple-element.53) | copy-start | bytes 2359300
  346.1 56.1 %collective-permute-start.1 = (bf16[1,128,2,8192]{1,3,2,0:T(8,128)(2,1)}, bf16[1,128,2,8192]{1,3,2,0:T(8,128)(2,1)}, u32[]{:S(2)}, u32[]{:S(2)}) collective-permute-start(bf16[1,128,2,8192]{1,3,2,0:T(8,128)(2,1)} %bitcast.115), channel_id=1, source_target_pairs={{32,0},{64,32},{96,64},{0,96},{33,1},{65,33},{97,65},{1,97},{34,2}... | collective-permute-start | bytes 12582920 | tf_op jit(solution)/shard_map/ppermute | solution.py:12
where the time goes:
time: 415 us; the launch traced here: 413 us
  waiting for transfers between devices  147 us (35%)
  matrix products  88.4 us (21%)
  local copies, waits for them, and re-layouts  80.6 us (19%)
  blocking collectives  52.8 us (13%)
  other arithmetic  26.2 us (6%)
  starting transfers between devices  17.1 us (4%)
    ppermute x2, waiting for transfers between devices, passed_along(): return lax.ppermute(block, axis, route)  94.6 us
    all_to_all x1, blocking collectives, collect_rows(): lax.all_to_all(shaped, ('seq', 'tp'), split_axis=0, concat_axis=3, tiled=...  52.8 us
    all_to_all x1, waiting for transfers between devices, spread_heads(): lax.all_to_all(shaped, ('seq', 'tp'), split_axis=3, concat_axis=0, tiled=...  52.5 us
    sub x3, matrix products, step(): raised = jnp.exp(scores - row_max)  30.9 us
    dot_general x3, matrix products, step(): jnp.einsum('bhd,shd->hbs', grad_block, values_all, preferred_element_type...  28.9 us
    unnamed x15, local copies, waits for them, and re-layouts  26.1 us
    convert_element_type x3, other arithmetic, step(): weights_low = weights.astype(jnp.bfloat16)  21 us
    all_to_all x1, local copies, waits for them, and re-layouts, collect_rows(): lax.all_to_all(shaped, ('seq', 'tp'), split_axis=0, concat_axis=3, tiled=...  11.2 us
  transfers between devices with their start and end apart: 3, of which 3 were waited for; matrix products, arithmetic and copies ran while one was open for 1% of the time, Pallas kernels for 0%

commit v1 on v0

v1 whole, which is shorter than its diff:
```python
import functools
import math

import jax
import jax.numpy as jnp
from jax import lax
from jax.experimental import pallas as pl
from jax.experimental.pallas import tpu as pltpu
from jax.sharding import PartitionSpec as P

MESH = pl.DeviceIdType.MESH
HEAD = 128
FACTOR = HEAD ** -0.5
LOG_SCALE = FACTOR * math.log2(math.e)
PIECES = 4
PARTS = 8
CHUNK = 512
UNROLL = 8
f32, bf16 = jnp.float32, jnp.bfloat16


def dot(a, b, ca, cb):
    return lax.dot_general(a, b, (((ca,), (cb,)), ((), ())), preferred_element_type=f32)


def split_rows():
    row = lax.broadcasted_iota(jnp.int32, (256, 256), 0)
    col = lax.broadcasted_iota(jnp.int32, (256, 256), 1)
    want = jnp.where(row < 128, 2 * row, 2 * row - 255)
    return (col == want).astype(bf16)


def kernel(
    groups, segments, tps,
    pairs, q_hbm, g_hbm, ctx_hbm, dq_hbm, out,
    kv, q_v, g_v, ctx_v, dq_v, kk, vv, kt, vt, s_scr, p_scr, acc,
    kv_send, kv_recv, g_send, g_recv, in_sem, out_sem,
):
    seg, sq, tp = lax.axis_index("segment"), lax.axis_index("seq"), lax.axis_index("tp")
    me = sq * tps + tp
    nxt, prv = lax.rem(seg + 1, segments), lax.rem(seg + segments - 1, segments)
    rows = pairs.shape[0]
    enc_len, dec_len = kk.shape[0], q_v.shape[0]
    heads = kv.shape[0]
    width = heads * HEAD
    part = rows // PIECES

    barrier = pltpu.get_barrier_semaphore()

    def greet(i, c):
        pl.semaphore_signal(barrier, inc=1, device_id=(prv, i // tps, lax.rem(i, tps)), device_id_type=MESH)
        return c

    lax.fori_loop(0, groups, greet, 0)
    pl.semaphore_wait(barrier, groups)

    def kv_copy(h, i, p):
        col = pl.multiple_of(i * width + h * HEAD, HEAD)
        piece = pl.ds(p * part, part)
        return pltpu.make_async_remote_copy(
            src_ref=pairs.at[piece, :, pl.ds(col, HEAD)], dst_ref=kv.at[h, me, piece],
            send_sem=kv_send.at[h], recv_sem=kv_recv.at[h],
            device_id=(nxt, i // tps, lax.rem(i, tps)), device_id_type=MESH)

    def g_copy(h, i, p):
        col = pl.multiple_of(me * width + h * HEAD, HEAD)
        piece = pl.ds(p * part, part)
        return pltpu.make_async_remote_copy(
            src_ref=kv.at[h, i, piece], dst_ref=out.at[piece, :, pl.ds(col, HEAD)],
            send_sem=g_send.at[h], recv_sem=g_recv.at[h],
            device_id=(prv, i // tps, lax.rem(i, tps)), device_id_type=MESH)

    for h in range(heads):
        def send(k, c):
            kv_copy(h, lax.rem(me + k, groups), k // groups).start()
            return c
        lax.fori_loop(0, groups * PIECES, send, 0)
    loads = [pltpu.make_async_copy(q_hbm, q_v, in_sem.at[0]), pltpu.make_async_copy(g_hbm, g_v, in_sem.at[1])]
    for load in loads:
        load.start()
    for load in loads:
        load.wait()

    sel = split_rows()
    sel_t = sel.T
    per = CHUNK // rows
    chunks = enc_len // CHUNK
    stores = []
    for h in range(heads):
        hs = slice(h * HEAD, (h + 1) * HEAD)
        flat = kv.at[h].reshape(groups, 2 * rows, HEAD)
        q, g = q_v.at[:, hs], g_v.at[:, hs]
        pltpu.make_async_copy(kv.at[h], kv.at[h], kv_recv.at[h]).wait()

        def split(i, c):
            for u in range(UNROLL):
                b = i * UNROLL + u
                y = dot(sel, flat[b], 1, 0).astype(bf16)
                r = pl.multiple_of(b * rows, rows)
                kk[pl.ds(r, rows), :] = y[:rows]
                vv[pl.ds(r, rows), :] = y[rows:]
                kt[:, pl.ds(r, rows)] = y[:rows].T
                vt[:, pl.ds(r, rows)] = y[rows:].T
            return c
        lax.fori_loop(0, groups // UNROLL, split, 0)

        def scores(i, m):
            o = pl.multiple_of(i * CHUNK, CHUNK)
            s = dot(kk[pl.ds(o, CHUNK), :], q[...], 1, 1)
            s_scr[pl.ds(o, CHUNK), :] = s
            return jnp.maximum(m, jnp.max(s.reshape(CHUNK // 8, 8, dec_len), axis=0))
        m = lax.fori_loop(0, chunks, scores, jnp.full((8, dec_len), -jnp.inf, f32))
        mc = jnp.max(m, axis=0, keepdims=True) * LOG_SCALE
        acc[...] = jnp.zeros_like(acc)

        def weigh(i, l):
            o = pl.multiple_of(i * CHUNK, CHUNK)
            p = jnp.exp2(s_scr[pl.ds(o, CHUNK), :] * LOG_SCALE - mc)
            pb = p.astype(bf16)
            p_scr[pl.ds(o, CHUNK), :] = pb
            acc[...] += dot(vt[:, pl.ds(o, CHUNK)], pb, 1, 0)
            return l + jnp.sum(p.reshape(CHUNK // 8, 8, dec_len), axis=0)
        l = lax.fori_loop(0, chunks, weigh, jnp.zeros((8, dec_len), f32))
        inv = 1.0 / jnp.sum(l, axis=0, keepdims=True)
        ctx = acc[...] * inv
        ctx_v[h] = ctx.T.astype(bf16)
        stores.append(pltpu.make_async_copy(ctx_v.at[h], ctx_hbm.at[:, hs], out_sem.at[0, h]))
        stores[-1].start()
        gf = g[...].astype(f32)
        row_dot = jnp.sum(gf.T * ctx, axis=0, keepdims=True)
        inv_col = jnp.broadcast_to(inv, (HEAD, dec_len)).T
        gn = (gf * inv_col).astype(bf16)
        qn = (q[...].astype(f32) * (inv_col * FACTOR)).astype(bf16)
        acc[...] = jnp.zeros_like(acc)

        def grads(i, c):
            chunk = lax.rem(i + me // per, chunks)
            o = pl.multiple_of(chunk * CHUNK, CHUNK)
            gw = dot(vv[pl.ds(o, CHUNK), :], g[...], 1, 1)
            pb = p_scr[pl.ds(o, CHUNK), :]
            ds = (pb.astype(f32) * (gw - row_dot)).astype(bf16)
            acc[...] += dot(kt[:, pl.ds(o, CHUNK)], ds, 1, 0)
            dk = dot(ds, qn, 1, 0).astype(bf16)
            dv = dot(pb, gn, 1, 0).astype(bf16)
            for u in range(per):
                a = u * rows
                x = jnp.concatenate([dk[a:a + rows], dv[a:a + rows]], axis=0)
                flat[chunk * per + u] = dot(sel_t, x, 1, 0).astype(bf16)
            for p in range(PIECES):
                for u in range(per):
                    g_copy(h, chunk * per + u, p).start()
            return c
        lax.fori_loop(0, chunks, grads, 0)
        dq_v[h] = (acc[...] * (inv * FACTOR)).T.astype(bf16)
        stores.append(pltpu.make_async_copy(dq_v.at[h], dq_hbm.at[:, hs], out_sem.at[1, h]))
        stores[-1].start()

    for store in stores:
        store.wait()
    for h in range(heads):
        for sem in (kv_send, g_send, g_recv):
            pltpu.make_async_copy(kv.at[h], kv.at[h], sem.at[h]).wait()


def place(ctx, dq, grads, ctx_out, dq_out, grads_out, ctx_v, dq_v, grads_v, load_sem, store_sem):
    part = grads.shape[0] // PARTS
    routes = [(grads.at[pl.ds(i * part, part)], grads_v.at[pl.ds(i * part, part)], grads_out.at[pl.ds(i * part, part)]) for i in range(PARTS)]
    routes += [(ctx, ctx_v, ctx_out), (dq, dq_v, dq_out)]
    loads = [pltpu.make_async_copy(src, mid, load_sem.at[i]) for i, (src, mid, _) in enumerate(routes)]
    stores = [pltpu.make_async_copy(mid, dst, store_sem.at[i]) for i, (_, mid, dst) in enumerate(routes)]
    for load in loads:
        load.start()
    for load, store in zip(loads, stores):
        load.wait()
        store.start()
    for store in stores:
        store.wait()


def shards(pairs, queries, upstream):
    groups = lax.axis_size("seq") * lax.axis_size("tp")
    _, rows, _, columns = pairs.shape
    _, dec_len, width = queries.shape
    heads = width // HEAD
    enc_len = rows * groups
    hbm = pl.BlockSpec(memory_space=pl.ANY)
    outs = [
        jax.ShapeDtypeStruct((dec_len, width), bf16),
        jax.ShapeDtypeStruct((dec_len, width), bf16),
        jax.ShapeDtypeStruct((rows, 2, columns), bf16),
    ]
    made = pl.pallas_call(
        functools.partial(kernel, groups, lax.axis_size("segment"), lax.axis_size("tp")),
        out_shape=outs,
        in_specs=[hbm] * 3,
        out_specs=[hbm] * 3,
        scratch_shapes=[
            pltpu.VMEM((heads, groups, rows, 2, HEAD), bf16),
            pltpu.VMEM((dec_len, width), bf16),
            pltpu.VMEM((dec_len, width), bf16),
            pltpu.VMEM((heads, dec_len, HEAD), bf16),
            pltpu.VMEM((heads, dec_len, HEAD), bf16),
            pltpu.VMEM((enc_len, HEAD), bf16),
            pltpu.VMEM((enc_len, HEAD), bf16),
            pltpu.VMEM((HEAD, enc_len), bf16),
            pltpu.VMEM((HEAD, enc_len), bf16),
            pltpu.VMEM((enc_len, dec_len), f32),
            pltpu.VMEM((enc_len, dec_len), bf16),
            pltpu.VMEM((HEAD, dec_len), f32),
            pltpu.SemaphoreType.DMA((heads,)),
            pltpu.SemaphoreType.DMA((heads,)),
            pltpu.SemaphoreType.DMA((heads,)),
            pltpu.SemaphoreType.DMA((heads,)),
            pltpu.SemaphoreType.DMA((2,)),
            pltpu.SemaphoreType.DMA((2, heads)),
        ],
        compiler_params=pltpu.CompilerParams(collective_id=0, has_side_effects=True, vmem_limit_bytes=60 * 2**20),
    )(pairs[0], queries[0], upstream[0])
    context, grad_query, grad_pairs = pl.pallas_call(
        place,
        out_shape=outs,
        in_specs=[hbm] * 3,
        out_specs=[hbm] * 3,
        scratch_shapes=[pltpu.VMEM(o.shape, o.dtype) for o in outs] + [pltpu.SemaphoreType.DMA((PARTS + 2,))] * 2,
        compiler_params=pltpu.CompilerParams(vmem_limit_bytes=20 * 2**20),
    )(*made)
    return (context[None], grad_query[None], grad_pairs[None])


def solution(mesh):
    rows = P("segment", ("seq", "tp"), None, None)
    columns = P("segment", None, ("seq", "tp"))
    return jax.shard_map(
        shards,
        mesh=mesh,
        in_specs=(rows, columns, columns),
        out_specs=(columns, columns, rows),
        check_vma=False,
    )
```

time: 415 us -> 125 us (0.30)
  waiting for transfers between devices: 147 us -> 0 us
  Pallas kernels: 0 us -> 118 us
  matrix products: 88.4 us -> 0 us
  local copies, waits for them, and re-layouts: 80.6 us -> 4.45 us
  blocking collectives: 52.8 us -> 0 us
  other arithmetic: 26.2 us -> 0 us
  starting transfers between devices: 17.1 us -> 0 us
    pallas_call x0 -> x2, Pallas kernels: none -> 118 us  [the longest x1 115 us: shards(): pl.pallas_call(functools.partial(kernel, groups, lax.axis_size('segment')...]
    ppermute x2 -> x0, waiting for transfers between devices: 94.6 us -> none  [passed_along(): return lax.ppermute(block, axis, route)]
    dot_general x15 -> x0, matrix products: 57.5 us -> none  [the longest x3 28.9 us: step(): jnp.einsum('bhd,shd->hbs', grad_block, values_all, preferred_element_type...]
    all_to_all x1 -> x0, blocking collectives: 52.8 us -> none  [collect_rows(): lax.all_to_all(shaped, ('seq', 'tp'), split_axis=0, concat_axis=3, tiled=...]
    all_to_all x1 -> x0, waiting for transfers between devices: 52.5 us -> none  [spread_heads(): lax.all_to_all(shaped, ('seq', 'tp'), split_axis=3, concat_axis=0, tiled=...]
    sub x3 -> x0, matrix products: 30.9 us -> none  [step(): raised = jnp.exp(scores - row_max)]
    unnamed x15 -> x6, local copies, waits for them, and re-layouts: 26.1 us -> 4.45 us
    convert_element_type x3 -> x0, other arithmetic: 21 us -> none  [step(): weights_low = weights.astype(jnp.bfloat16)]
  transfers between devices with their start and end apart: 3 -> 0, of which waited for: 3 -> 0; matrix products, arithmetic and copies ran while one was open for 1% -> 0% of each run, Pallas kernels for 0% -> 0%
where the time goes in v1:
time: 125 us; the launch traced here: 123 us
  Pallas kernels  118 us (94%)
  local copies, waits for them, and re-layouts  4.45 us (4%)
    pallas_call x1, Pallas kernels, shards(): pl.pallas_call(functools.partial(kernel, groups, lax.axis_size('segment')...  115 us
    unnamed x6, local copies, waits for them, and re-layouts  4.45 us
    pallas_call x1, Pallas kernels, shards(): pl.pallas_call(place, out_shape=outs, in_specs=[hbm] * 3, out_specs=[hbm]...  3.06 us

profile of v1, /device:TPU:1, one launch (start us, length us, event | category | flops | bytes accessed | tf_op | source)
XLA Modules:
  0.0 122.7 jit_solution(16331865297681250113)
XLA Ops:
  0.6 114.6 %shard_map.58 = (bf16[1536,256]{1,0:T(8,128)(2,1)}, bf16[1536,256]{1,0:T(8,128)(2,1)}, bf16[128,2,8192]{2,1,0:T(2,128)(2,1)}) custom-call(bf16[128,2,8192]{2,1,0:T(2,128)(2,1)} %bitcast.6, bf16[1536,256]{1,0:T(8,128)(2,1)} %bitcast.7, bf16[1536,256]{1,0:T(8,128)(2,1)} %bitcast.8), custom_call_target="tpu_custom_call" | custom-call | tf_op jit(solution)/shard_map/pallas_call | solution.py:192
  115.2 0.0 copy-start
  115.2 2.2 %copy-done = bf16[128,2,8192]{2,1,0:T(2,128)(2,1)S(1)} copy-done((bf16[128,2,8192]{2,1,0:T(2,128)(2,1)S(1)}, bf16[128,2,8192]{2,1,0:T(2,128)(2,1)}, u32[]{:S(2)}) %copy-start) | copy-done | bytes 4194328
  117.4 0.0 copy-start.1
  117.4 1.1 copy-done.1
  118.6 0.0 copy-start.2
  118.6 1.1 copy-done.2
  119.7 3.1 %shard_map.59 = (bf16[1536,256]{1,0:T(8,128)(2,1)}, bf16[1536,256]{1,0:T(8,128)(2,1)}, bf16[128,2,8192]{2,1,0:T(2,128)(2,1)}) custom-call(bf16[1536,256]{1,0:T(8,128)(2,1)S(1)} %copy-done.1, bf16[1536,256]{1,0:T(8,128)(2,1)S(1)} %copy-done.2, bf16[128,2,8192]{2,1,0:T(2,128)(2,1)S(1)} %copy-done), custom_call_target="tpu_custom_call" | custom-call | tf_op jit(solution)/shard_map/pallas_call | solution.py:219
Async XLA Ops:
  115.2 2.2 %copy-start = (bf16[128,2,8192]{2,1,0:T(2,128)(2,1)S(1)}, bf16[128,2,8192]{2,1,0:T(2,128)(2,1)}, u32[]{:S(2)}) copy-start(bf16[128,2,8192]{2,1,0:T(2,128)(2,1)} %get-tuple-element.11.grads) | copy-start | bytes 12582916
  117.4 1.1 copy-start.1
  118.6 1.1 copy-start.2

commit v2 on v1

--- a/solution.py
+++ b/solution.py
@@ -12,8 +12,9 @@
 HEAD = 128
 FACTOR = HEAD ** -0.5
 LOG_SCALE = FACTOR * math.log2(math.e)
-PIECES = 4
+PIECES = 2
 PARTS = 8
+BATCH = 1
 CHUNK = 512
 UNROLL = 8
 f32, bf16 = jnp.float32, jnp.bfloat16
@@ -28,6 +29,20 @@
     col = lax.broadcasted_iota(jnp.int32, (256, 256), 1)
     want = jnp.where(row < 128, 2 * row, 2 * row - 255)
     return (col == want).astype(bf16)
+
+
+def spread(pos, sq, tp):
+    j = lax.rem(5 * lax.rem(pos, 16) + 3, 16)
+    dz, dx = j // 4, lax.rem(j, 4)
+    z, x = lax.rem(sq // 4 + dz, 4), lax.rem(lax.rem(sq, 4) + dx, 4)
+    return z * 4 + x, lax.rem(tp + dz + dx + pos // 16, 2)
+
+
+def seen_from(pos):
+    j = lax.rem(5 * lax.rem(pos, 16) + 3, 16)
+    dz, dx = j // 4, lax.rem(j, 4)
+    back = lax.rem(4 - dz, 4) * 4 + lax.rem(4 - dx, 4)
+    return (pos // 16) * 16 + lax.rem((back + 13) * 13, 16)
 
 
 def kernel(
@@ -54,25 +69,27 @@
     lax.fori_loop(0, groups, greet, 0)
     pl.semaphore_wait(barrier, groups)
 
-    def kv_copy(h, i, p):
-        col = pl.multiple_of(i * width + h * HEAD, HEAD)
+    def kv_copy(h, pos, p):
+        to_sq, to_tp = spread(pos, sq, tp)
+        col = pl.multiple_of((to_sq * tps + to_tp) * width + h * HEAD, HEAD)
         piece = pl.ds(p * part, part)
         return pltpu.make_async_remote_copy(
-            src_ref=pairs.at[piece, :, pl.ds(col, HEAD)], dst_ref=kv.at[h, me, piece],
+            src_ref=pairs.at[piece, :, pl.ds(col, HEAD)], dst_ref=kv.at[h, seen_from(pos), piece],
             send_sem=kv_send.at[h], recv_sem=kv_recv.at[h],
-            device_id=(nxt, i // tps, lax.rem(i, tps)), device_id_type=MESH)
-
-    def g_copy(h, i, p):
+            device_id=(nxt, to_sq, to_tp), device_id_type=MESH)
+
+    def g_copy(h, pos, p):
+        to_sq, to_tp = spread(pos, sq, tp)
         col = pl.multiple_of(me * width + h * HEAD, HEAD)
         piece = pl.ds(p * part, part)
         return pltpu.make_async_remote_copy(
-            src_ref=kv.at[h, i, piece], dst_ref=out.at[piece, :, pl.ds(col, HEAD)],
+            src_ref=kv.at[h, pos, piece], dst_ref=out.at[piece, :, pl.ds(col, HEAD)],
             send_sem=g_send.at[h], recv_sem=g_recv.at[h],
-            device_id=(prv, i // tps, lax.rem(i, tps)), device_id_type=MESH)
+            device_id=(prv, to_sq, to_tp), device_id_type=MESH)
 
     for h in range(heads):
         def send(k, c):
-            kv_copy(h, lax.rem(me + k, groups), k // groups).start()
+            kv_copy(h, lax.rem(k, groups), k // groups).start()
             return c
         lax.fori_loop(0, groups * PIECES, send, 0)
     loads = [pltpu.make_async_copy(q_hbm, q_v, in_sem.at[0]), pltpu.make_async_copy(g_hbm, g_v, in_sem.at[1])]
@@ -134,8 +151,7 @@
         acc[...] = jnp.zeros_like(acc)
 
         def grads(i, c):
-            chunk = lax.rem(i + me // per, chunks)
-            o = pl.multiple_of(chunk * CHUNK, CHUNK)
+            o = pl.multiple_of(i * CHUNK, CHUNK)
             gw = dot(vv[pl.ds(o, CHUNK), :], g[...], 1, 1)
             pb = p_scr[pl.ds(o, CHUNK), :]
             ds = (pb.astype(f32) * (gw - row_dot)).astype(bf16)
@@ -145,10 +161,14 @@
             for u in range(per):
                 a = u * rows
                 x = jnp.concatenate([dk[a:a + rows], dv[a:a + rows]], axis=0)
-                flat[chunk * per + u] = dot(sel_t, x, 1, 0).astype(bf16)
-            for p in range(PIECES):
-                for u in range(per):
-                    g_copy(h, chunk * per + u, p).start()
+                flat[i * per + u] = dot(sel_t, x, 1, 0).astype(bf16)
+
+            @pl.when(lax.rem(i + 1, BATCH) == 0)
+            def _():
+                def send(k, c):
+                    g_copy(h, (i + 1 - BATCH) * per + lax.rem(k, BATCH * per), k // (BATCH * per)).start()
+                    return c
+                lax.fori_loop(0, BATCH * per * PIECES, send, 0)
             return c
         lax.fori_loop(0, chunks, grads, 0)
         dq_v[h] = (acc[...] * (inv * FACTOR)).T.astype(bf16)
@@ -162,19 +182,15 @@
             pltpu.make_async_copy(kv.at[h], kv.at[h], sem.at[h]).wait()
 
 
-def place(ctx, dq, grads, ctx_out, dq_out, grads_out, ctx_v, dq_v, grads_v, load_sem, store_sem):
-    part = grads.shape[0] // PARTS
-    routes = [(grads.at[pl.ds(i * part, part)], grads_v.at[pl.ds(i * part, part)], grads_out.at[pl.ds(i * part, part)]) for i in range(PARTS)]
-    routes += [(ctx, ctx_v, ctx_out), (dq, dq_v, dq_out)]
-    loads = [pltpu.make_async_copy(src, mid, load_sem.at[i]) for i, (src, mid, _) in enumerate(routes)]
-    stores = [pltpu.make_async_copy(mid, dst, store_sem.at[i]) for i, (_, mid, dst) in enumerate(routes)]
-    for load in loads:
-        load.start()
-    for load, store in zip(loads, stores):
-        load.wait()
-        store.start()
-    for store in stores:
-        store.wait()
+def place(ctx, dq, grads, ctx_out, dq_out, grads_out, sem):
+    copies = [
+        pltpu.make_async_copy(src, dst, sem.at[i])
+        for i, (src, dst) in enumerate(((grads, grads_out), (ctx, ctx_out), (dq, dq_out)))
+    ]
+    for copy in copies:
+        copy.start()
+    for copy in copies:
+        copy.wait()
 
 
 def shards(pairs, queries, upstream):
@@ -191,7 +207,7 @@
     ]
     made = pl.pallas_call(
         functools.partial(kernel, groups, lax.axis_size("segment"), lax.axis_size("tp")),
-        out_shape=outs,
+        out_shape=[pltpu.VMEM(o.shape, o.dtype) for o in outs],
         in_specs=[hbm] * 3,
         out_specs=[hbm] * 3,
         scratch_shapes=[
@@ -214,14 +230,14 @@
             pltpu.SemaphoreType.DMA((2,)),
             pltpu.SemaphoreType.DMA((2, heads)),
         ],
-        compiler_params=pltpu.CompilerParams(collective_id=0, has_side_effects=True, vmem_limit_bytes=60 * 2**20),
+        compiler_params=pltpu.CompilerParams(collective_id=0, has_side_effects=True, vmem_limit_bytes=54 * 2**20),
     )(pairs[0], queries[0], upstream[0])
     context, grad_query, grad_pairs = pl.pallas_call(
         place,
         out_shape=outs,
-        in_specs=[hbm] * 3,
+        in_specs=[pl.BlockSpec(memory_space=pltpu.VMEM)] * 3,
         out_specs=[hbm] * 3,
-        scratch_shapes=[pltpu.VMEM(o.shape, o.dtype) for o in outs] + [pltpu.SemaphoreType.DMA((PARTS + 2,))] * 2,
+        scratch_shapes=[pltpu.SemaphoreType.DMA((3,))],
         compiler_params=pltpu.CompilerParams(vmem_limit_bytes=20 * 2**20),
     )(*made)
     return (context[None], grad_query[None], grad_pairs[None])

time: 125 us -> 115 us (0.920); the launches traced: 123 us -> 115 us
  local copies, waits for them, and re-layouts: 4.45 us -> 0 us
  Pallas kernels: 118 us -> 115 us
    unnamed x6 -> x0, local copies, waits for them, and re-layouts: 4.45 us -> none
    pallas_call x1, Pallas kernels: 115 us -> 112 us  [shards(): pl.pallas_call(functools.partial(kernel, groups, lax.axis_size('segment')...]
where the time goes in v2:
time: 115 us
  Pallas kernels  115 us (100%)
    pallas_call x1, Pallas kernels, shards(): pl.pallas_call(functools.partial(kernel, groups, lax.axis_size('segment')...  112 us
    pallas_call x1, Pallas kernels, shards(): pl.pallas_call(place, out_shape=outs, in_specs=[pl.BlockSpec(memory_space...  2.52 us

profile of v2, /device:TPU:1, one launch (start us, length us, event | category | flops | bytes accessed | tf_op | source)
XLA Modules:
  0.0 115.3 jit_solution(11389068578264283103)
XLA Ops:
  0.6 112.1 %shard_map.58 = (bf16[1536,256]{1,0:T(8,128)(2,1)S(1)}, bf16[1536,256]{1,0:T(8,128)(2,1)S(1)}, bf16[128,2,8192]{2,1,0:T(2,128)(2,1)S(1)}) custom-call(bf16[128,2,8192]{2,1,0:T(2,128)(2,1)} %bitcast.6, bf16[1536,256]{1,0:T(8,128)(2,1)} %bitcast.7, bf16[1536,256]{1,0:T(8,128)(2,1)} %bitcast.8), custom_call_target="tpu_custom_call" | custom-call | tf_op jit(solution)/shard_map/pallas_call | solution.py:208
  112.7 2.5 %shard_map.59 = (bf16[1536,256]{1,0:T(8,128)(2,1)}, bf16[1536,256]{1,0:T(8,128)(2,1)}, bf16[128,2,8192]{2,1,0:T(2,128)(2,1)}) custom-call(bf16[1536,256]{1,0:T(8,128)(2,1)S(1)} %get-tuple-element.9.ctx, bf16[1536,256]{1,0:T(8,128)(2,1)S(1)} %get-tuple-element.10.dq, bf16[128,2,8192]{2,1,0:T(2,128)(2,1)S(1)} %get-tuple-element.11.grads), custom_call_target="tpu_custom_call" | custom-call | tf_op jit(solution)/shard_map/pallas_call | solution.py:235

commit v3 on v2

--- a/solution.py
+++ b/solution.py
@@ -13,10 +13,8 @@
 FACTOR = HEAD ** -0.5
 LOG_SCALE = FACTOR * math.log2(math.e)
 PIECES = 2
-PARTS = 8
-BATCH = 1
+HALF = 16
 CHUNK = 512
-UNROLL = 8
 f32, bf16 = jnp.float32, jnp.bfloat16
 
 
@@ -48,14 +46,14 @@
 def kernel(
     groups, segments, tps,
     pairs, q_hbm, g_hbm, ctx_hbm, dq_hbm, out,
-    kv, q_v, g_v, ctx_v, dq_v, kk, vv, kt, vt, s_scr, p_scr, acc,
+    kv, q_v, g_v, ctx_v, dq_v, vv, kt, vt, s_scr, p_scr, acc,
     kv_send, kv_recv, g_send, g_recv, in_sem, out_sem,
 ):
     seg, sq, tp = lax.axis_index("segment"), lax.axis_index("seq"), lax.axis_index("tp")
     me = sq * tps + tp
     nxt, prv = lax.rem(seg + 1, segments), lax.rem(seg + segments - 1, segments)
     rows = pairs.shape[0]
-    enc_len, dec_len = kk.shape[0], q_v.shape[0]
+    enc_len, dec_len = vv.shape[0], q_v.shape[0]
     heads = kv.shape[0]
     width = heads * HEAD
     part = rows // PIECES
@@ -75,21 +73,22 @@
         piece = pl.ds(p * part, part)
         return pltpu.make_async_remote_copy(
             src_ref=pairs.at[piece, :, pl.ds(col, HEAD)], dst_ref=kv.at[h, seen_from(pos), piece],
-            send_sem=kv_send.at[h], recv_sem=kv_recv.at[h],
+            send_sem=kv_send.at[h], recv_sem=kv_recv.at[h, pos // HALF],
             device_id=(nxt, to_sq, to_tp), device_id_type=MESH)
 
-    def g_copy(h, pos, p):
+    def g_copies(h, pos):
         to_sq, to_tp = spread(pos, sq, tp)
         col = pl.multiple_of(me * width + h * HEAD, HEAD)
-        piece = pl.ds(p * part, part)
-        return pltpu.make_async_remote_copy(
+        pieces = [pl.ds(p * part, part) for p in range(PIECES)]
+        return [pltpu.make_async_remote_copy(
             src_ref=kv.at[h, pos, piece], dst_ref=out.at[piece, :, pl.ds(col, HEAD)],
             send_sem=g_send.at[h], recv_sem=g_recv.at[h],
-            device_id=(prv, to_sq, to_tp), device_id_type=MESH)
+            device_id=(prv, to_sq, to_tp), device_id_type=MESH) for piece in pieces]
 
     for h in range(heads):
         def send(k, c):
-            kv_copy(h, lax.rem(k, groups), k // groups).start()
+            half, inner = k // (HALF * PIECES), lax.rem(k, HALF * PIECES)
+            kv_copy(h, half * HALF + lax.rem(inner, HALF), inner // HALF).start()
             return c
         lax.fori_loop(0, groups * PIECES, send, 0)
     loads = [pltpu.make_async_copy(q_hbm, q_v, in_sem.at[0]), pltpu.make_async_copy(g_hbm, g_v, in_sem.at[1])]
@@ -98,6 +97,7 @@
     for load in loads:
         load.wait()
 
+    vt[HEAD:, :] = jnp.ones((16, enc_len), bf16)
     sel = split_rows()
     sel_t = sel.T
     per = CHUNK // rows
@@ -107,39 +107,37 @@
         hs = slice(h * HEAD, (h + 1) * HEAD)
         flat = kv.at[h].reshape(groups, 2 * rows, HEAD)
         q, g = q_v.at[:, hs], g_v.at[:, hs]
-        pltpu.make_async_copy(kv.at[h], kv.at[h], kv_recv.at[h]).wait()
-
-        def split(i, c):
-            for u in range(UNROLL):
-                b = i * UNROLL + u
-                y = dot(sel, flat[b], 1, 0).astype(bf16)
-                r = pl.multiple_of(b * rows, rows)
-                kk[pl.ds(r, rows), :] = y[:rows]
+
+        def scores(i, m):
+            o = pl.multiple_of(i * CHUNK, CHUNK)
+            keys = []
+            for u in range(per):
+                y = dot(sel, flat[i * per + u], 1, 0).astype(bf16)
+                r = pl.multiple_of(o + u * rows, rows)
+                keys.append(y[:rows])
                 vv[pl.ds(r, rows), :] = y[rows:]
                 kt[:, pl.ds(r, rows)] = y[:rows].T
-                vt[:, pl.ds(r, rows)] = y[rows:].T
-            return c
-        lax.fori_loop(0, groups // UNROLL, split, 0)
-
-        def scores(i, m):
-            o = pl.multiple_of(i * CHUNK, CHUNK)
-            s = dot(kk[pl.ds(o, CHUNK), :], q[...], 1, 1)
+                vt[:HEAD, pl.ds(r, rows)] = y[rows:].T
+            s = dot(jnp.concatenate(keys, axis=0), q[...], 1, 1)
             s_scr[pl.ds(o, CHUNK), :] = s
             return jnp.maximum(m, jnp.max(s.reshape(CHUNK // 8, 8, dec_len), axis=0))
-        m = lax.fori_loop(0, chunks, scores, jnp.full((8, dec_len), -jnp.inf, f32))
+        m = jnp.full((8, dec_len), -jnp.inf, f32)
+        for half in range(groups // HALF):
+            arrived = kv.at[h, pl.ds(half * HALF, HALF)]
+            pltpu.make_async_copy(arrived, arrived, kv_recv.at[h, half]).wait()
+            m = lax.fori_loop(half * HALF // per, (half + 1) * HALF // per, scores, m)
         mc = jnp.max(m, axis=0, keepdims=True) * LOG_SCALE
         acc[...] = jnp.zeros_like(acc)
 
-        def weigh(i, l):
+        def weigh(i, c):
             o = pl.multiple_of(i * CHUNK, CHUNK)
-            p = jnp.exp2(s_scr[pl.ds(o, CHUNK), :] * LOG_SCALE - mc)
-            pb = p.astype(bf16)
+            pb = jnp.exp2(s_scr[pl.ds(o, CHUNK), :] * LOG_SCALE - mc).astype(bf16)
             p_scr[pl.ds(o, CHUNK), :] = pb
             acc[...] += dot(vt[:, pl.ds(o, CHUNK)], pb, 1, 0)
-            return l + jnp.sum(p.reshape(CHUNK // 8, 8, dec_len), axis=0)
-        l = lax.fori_loop(0, chunks, weigh, jnp.zeros((8, dec_len), f32))
-        inv = 1.0 / jnp.sum(l, axis=0, keepdims=True)
-        ctx = acc[...] * inv
+            return c
+        lax.fori_loop(0, chunks, weigh, 0)
+        inv = 1.0 / acc[HEAD:HEAD + 1, :]
+        ctx = acc[:HEAD, :] * inv
         ctx_v[h] = ctx.T.astype(bf16)
         stores.append(pltpu.make_async_copy(ctx_v.at[h], ctx_hbm.at[:, hs], out_sem.at[0, h]))
         stores[-1].start()
@@ -148,14 +146,14 @@
         inv_col = jnp.broadcast_to(inv, (HEAD, dec_len)).T
         gn = (gf * inv_col).astype(bf16)
         qn = (q[...].astype(f32) * (inv_col * FACTOR)).astype(bf16)
-        acc[...] = jnp.zeros_like(acc)
+        acc[:HEAD, :] = jnp.zeros((HEAD, dec_len), f32)
 
         def grads(i, c):
             o = pl.multiple_of(i * CHUNK, CHUNK)
             gw = dot(vv[pl.ds(o, CHUNK), :], g[...], 1, 1)
             pb = p_scr[pl.ds(o, CHUNK), :]
             ds = (pb.astype(f32) * (gw - row_dot)).astype(bf16)
-            acc[...] += dot(kt[:, pl.ds(o, CHUNK)], ds, 1, 0)
+            acc[:HEAD, :] += dot(kt[:, pl.ds(o, CHUNK)], ds, 1, 0)
             dk = dot(ds, qn, 1, 0).astype(bf16)
             dv = dot(pb, gn, 1, 0).astype(bf16)
             for u in range(per):
@@ -163,15 +161,12 @@
                 x = jnp.concatenate([dk[a:a + rows], dv[a:a + rows]], axis=0)
                 flat[i * per + u] = dot(sel_t, x, 1, 0).astype(bf16)
 
-            @pl.when(lax.rem(i + 1, BATCH) == 0)
-            def _():
-                def send(k, c):
-                    g_copy(h, (i + 1 - BATCH) * per + lax.rem(k, BATCH * per), k // (BATCH * per)).start()
-                    return c
-                lax.fori_loop(0, BATCH * per * PIECES, send, 0)
+            for u in range(per):
+                for copy in g_copies(h, i * per + u):
+                    copy.start()
             return c
         lax.fori_loop(0, chunks, grads, 0)
-        dq_v[h] = (acc[...] * (inv * FACTOR)).T.astype(bf16)
+        dq_v[h] = (acc[:HEAD, :] * (inv * FACTOR)).T.astype(bf16)
         stores.append(pltpu.make_async_copy(dq_v.at[h], dq_hbm.at[:, hs], out_sem.at[1, h]))
         stores[-1].start()
 
@@ -217,14 +212,13 @@
             pltpu.VMEM((heads, dec_len, HEAD), bf16),
             pltpu.VMEM((heads, dec_len, HEAD), bf16),
             pltpu.VMEM((enc_len, HEAD), bf16),
-            pltpu.VMEM((enc_len, HEAD), bf16),
             pltpu.VMEM((HEAD, enc_len), bf16),
-            pltpu.VMEM((HEAD, enc_len), bf16),
+            pltpu.VMEM((HEAD + 16, enc_len), bf16),
             pltpu.VMEM((enc_len, dec_len), f32),
             pltpu.VMEM((enc_len, dec_len), bf16),
-            pltpu.VMEM((HEAD, dec_len), f32),
+            pltpu.VMEM((HEAD + 16, dec_len), f32),
             pltpu.SemaphoreType.DMA((heads,)),
-            pltpu.SemaphoreType.DMA((heads,)),
+            pltpu.SemaphoreType.DMA((heads, groups // HALF)),
             pltpu.SemaphoreType.DMA((heads,)),
             pltpu.SemaphoreType.DMA((heads,)),
             pltpu.SemaphoreType.DMA((2,)),

time: 115 us -> 112 us (0.974)
  Pallas kernels: 115 us -> 111 us
    pallas_call x1, Pallas kernels: 112 us -> 109 us  [shards(): pl.pallas_call(functools.partial(kernel, groups, lax.axis_size('segment')...]
where the time goes in v3:
time: 112 us
  Pallas kernels  111 us (99%)
    pallas_call x1, Pallas kernels, shards(): pl.pallas_call(functools.partial(kernel, groups, lax.axis_size('segment')...  109 us
    pallas_call x1, Pallas kernels, shards(): pl.pallas_call(place, out_shape=outs, in_specs=[pl.BlockSpec(memory_space...  2.52 us

profile of v3, /device:TPU:1, one launch (start us, length us, event | category | flops | bytes accessed | tf_op | source)
XLA Modules:
  0.0 111.7 jit_solution(6216767704520492297)
XLA Ops:
  0.6 108.6 %shard_map.58 = (bf16[1536,256]{1,0:T(8,128)(2,1)S(1)}, bf16[1536,256]{1,0:T(8,128)(2,1)S(1)}, bf16[128,2,8192]{2,1,0:T(2,128)(2,1)S(1)}) custom-call(bf16[128,2,8192]{2,1,0:T(2,128)(2,1)} %bitcast.6, bf16[1536,256]{1,0:T(8,128)(2,1)} %bitcast.7, bf16[1536,256]{1,0:T(8,128)(2,1)} %bitcast.8), custom_call_target="tpu_custom_call" | custom-call | tf_op jit(solution)/shard_map/pallas_call | solution.py:203
  109.2 2.5 %shard_map.59 = (bf16[1536,256]{1,0:T(8,128)(2,1)}, bf16[1536,256]{1,0:T(8,128)(2,1)}, bf16[128,2,8192]{2,1,0:T(2,128)(2,1)}) custom-call(bf16[1536,256]{1,0:T(8,128)(2,1)S(1)} %get-tuple-element.9.ctx, bf16[1536,256]{1,0:T(8,128)(2,1)S(1)} %get-tuple-element.10.dq, bf16[128,2,8192]{2,1,0:T(2,128)(2,1)S(1)} %get-tuple-element.11.grads), custom_call_target="tpu_custom_call" | custom-call | tf_op jit(solution)/shard_map/pallas_call | solution.py:229

commit v4 on v3

--- a/solution.py
+++ b/solution.py
@@ -13,7 +13,8 @@
 FACTOR = HEAD ** -0.5
 LOG_SCALE = FACTOR * math.log2(math.e)
 PIECES = 2
-HALF = 16
+IN_PIECES = 4
+HALF = 32
 CHUNK = 512
 f32, bf16 = jnp.float32, jnp.bfloat16
 
@@ -57,6 +58,7 @@
     heads = kv.shape[0]
     width = heads * HEAD
     part = rows // PIECES
+    in_part = rows // IN_PIECES
 
     barrier = pltpu.get_barrier_semaphore()
 
@@ -70,7 +72,7 @@
     def kv_copy(h, pos, p):
         to_sq, to_tp = spread(pos, sq, tp)
         col = pl.multiple_of((to_sq * tps + to_tp) * width + h * HEAD, HEAD)
-        piece = pl.ds(p * part, part)
+        piece = pl.ds(p * in_part, in_part)
         return pltpu.make_async_remote_copy(
             src_ref=pairs.at[piece, :, pl.ds(col, HEAD)], dst_ref=kv.at[h, seen_from(pos), piece],
             send_sem=kv_send.at[h], recv_sem=kv_recv.at[h, pos // HALF],
@@ -87,10 +89,10 @@
 
     for h in range(heads):
         def send(k, c):
-            half, inner = k // (HALF * PIECES), lax.rem(k, HALF * PIECES)
+            half, inner = k // (HALF * IN_PIECES), lax.rem(k, HALF * IN_PIECES)
             kv_copy(h, half * HALF + lax.rem(inner, HALF), inner // HALF).start()
             return c
-        lax.fori_loop(0, groups * PIECES, send, 0)
+        lax.fori_loop(0, groups * IN_PIECES, send, 0)
     loads = [pltpu.make_async_copy(q_hbm, q_v, in_sem.at[0]), pltpu.make_async_copy(g_hbm, g_v, in_sem.at[1])]
     for load in loads:
         load.start()

time: 112 us -> 113 us (level)
  Pallas kernels: 111 us -> 113 us
    pallas_call x1, Pallas kernels: 109 us -> 110 us  [shards(): pl.pallas_call(functools.partial(kernel, groups, lax.axis_size('segment')...]
where the time goes in v4:
time: 113 us
  Pallas kernels  113 us (100%)
    pallas_call x1, Pallas kernels, shards(): pl.pallas_call(functools.partial(kernel, groups, lax.axis_size('segment')...  110 us
    pallas_call x1, Pallas kernels, shards(): pl.pallas_call(place, out_shape=outs, in_specs=[pl.BlockSpec(memory_space...  2.52 us

profile of v4, /device:TPU:1, one launch (start us, length us, event | category | flops | bytes accessed | tf_op | source)
XLA Modules:
  0.0 113.3 jit_solution(11433462270065000980)
XLA Ops:
  0.6 110.1 %shard_map.58 = (bf16[1536,256]{1,0:T(8,128)(2,1)S(1)}, bf16[1536,256]{1,0:T(8,128)(2,1)S(1)}, bf16[128,2,8192]{2,1,0:T(2,128)(2,1)S(1)}) custom-call(bf16[128,2,8192]{2,1,0:T(2,128)(2,1)} %bitcast.6, bf16[1536,256]{1,0:T(8,128)(2,1)} %bitcast.7, bf16[1536,256]{1,0:T(8,128)(2,1)} %bitcast.8), custom_call_target="tpu_custom_call" | custom-call | tf_op jit(solution)/shard_map/pallas_call | solution.py:205
  110.8 2.5 %shard_map.59 = (bf16[1536,256]{1,0:T(8,128)(2,1)}, bf16[1536,256]{1,0:T(8,128)(2,1)}, bf16[128,2,8192]{2,1,0:T(2,128)(2,1)}) custom-call(bf16[1536,256]{1,0:T(8,128)(2,1)S(1)} %get-tuple-element.9.ctx, bf16[1536,256]{1,0:T(8,128)(2,1)S(1)} %get-tuple-element.10.dq, bf16[128,2,8192]{2,1,0:T(2,128)(2,1)S(1)} %get-tuple-element.11.grads), custom_call_target="tpu_custom_call" | custom-call | tf_op jit(solution)/shard_map/pallas_call | solution.py:231
